TPU v7x, 32 devices: a whole 2x2x4 slice. The times are simulated.
32 devices in a mesh: groups: 2 (over y), chan: 4 (over z), space: 4 (over x, core).
Axes of the slice: x: 2, y: 2, z: 4, core: 2. Of those that a mesh axis runs over, the one named last changes fastest.
Arguments:
- volume: bfloat16 [2048, 16, 512], P(('groups', 'chan'), 'space'), parts along dimension 0, may hold values from -6 to 6
- out_grad: bfloat16 [2048, 16, 512], P(('groups', 'chan'), 'space'), parts along dimension 0, may hold values from -6 to 6
- weight_in: bfloat16 [1024, 1024], P('chan'), may hold values from -0.1875 to 0.1875
- weight_out: bfloat16 [1024, 1024], P('chan'), may hold values from -0.1875 to 0.1875
- filter_taps: float32 [1024, 27], P('chan'), may hold values from -1.25 to 1.25
- filter_bias: float32 [1024], P('chan'), may hold values from -3 to 3
Outputs:
- block_out: bfloat16 [2048, 16, 512], P(('groups', 'chan'), 'space'), parts along dimension 0
- volume_grad: bfloat16 [2048, 16, 512], P(('groups', 'chan'), 'space'), parts along dimension 0
There are 2 independent parts, one for each index of `groups`. A program takes and returns all parts, laid end to end along the dimension named above; an argument that names none is the same for every part. Nothing has to cross between parts.
All inputs are finite; a program needn't handle non-finite values.
Results may differ from a plain program's by a relative error of at most 0.0085.
Values may be sent and summed in bfloat16 or wider, within the bound.
A program may use at most 64 MiB of HBM per device.

v0:
```python
import jax
import jax.numpy as jnp
from jax import lax
from jax.sharding import PartitionSpec as P

CX = 32
CY = 16


root_half = 0.7071067811865476
inv_root_two_pi = 0.3989422804014327


def with_halo(block, sides, width):
    for axis, dim in sides:
        count = lax.axis_size(axis)
        forward = [(i, i + 1) for i in range(count - 1)]
        backward = [(target, source) for source, target in forward]
        low = lax.ppermute(
            lax.slice_in_dim(block, block.shape[dim] - width, None, axis=dim), axis, forward
        )
        high = lax.ppermute(lax.slice_in_dim(block, 0, width, axis=dim), axis, backward)
        block = jnp.concatenate([low, block, high], axis=dim)
    return block


def gelu_value(field):
    return 0.5 * field * (1.0 + lax.erf(field * root_half))


def gelu_slope(field):
    return (
        0.5 * (1.0 + lax.erf(field * root_half))
        + field * jnp.exp(-0.5 * field * field) * inv_root_two_pi
    )


def core(padded, filter_taps, direction):
    extent_z = padded.shape[1] - 2
    extent_y = padded.shape[2] - 2
    extent_x = padded.shape[3] - 2
    summed = jnp.zeros((padded.shape[0], extent_z, extent_y, extent_x), jnp.float32)
    for shift_z in range(3):
        for shift_y in range(3):
            for shift_x in range(3):
                tap_index = (shift_z * 3 + shift_y) * 3 + shift_x
                begin_z = 1 + direction * (shift_z - 1)
                begin_y = 1 + direction * (shift_y - 1)
                begin_x = 1 + direction * (shift_x - 1)
                window = padded[
                    :,
                    begin_z : begin_z + extent_z,
                    begin_y : begin_y + extent_y,
                    begin_x : begin_x + extent_x,
                ]
                summed = summed + filter_taps[:, tap_index][:, None, None, None] * window
    return summed


def lift(field_z):
    extended = field_z.astype(jnp.float32).reshape(field_z.shape[0], field_z.shape[1], CY, CX)
    return jnp.pad(extended, ((0, 0), (0, 0), (1, 1), (1, 1)))


def to_cells(field):
    return lax.all_to_all(
        field.reshape(field.shape[0], -1), "chan", split_axis=1, concat_axis=0, tiled=True
    )


def to_channels(field, slab_shape):
    return lax.all_to_all(field, "chan", split_axis=0, concat_axis=1, tiled=True).reshape(
        slab_shape
    )


def body(volume, out_grad, weight_in, weight_out, filter_taps, filter_bias):
    slab_shape = volume.shape
    contract_first = (((0,), (0,)), ((), ()))
    full_in, full_out = (
        lax.all_gather(weight_in, "chan", axis=0, tiled=True),
        lax.all_gather(weight_out, "chan", axis=0, tiled=True),
    )
    vol_cells = to_cells(volume)
    hidden = to_channels(
        jnp.dot(full_in, vol_cells, preferred_element_type=jnp.float32).astype(jnp.bfloat16),
        slab_shape,
    )
    padded = lift(with_halo(hidden, (("space", 1),), 1))
    mixed = core(padded, filter_taps, 1) + filter_bias[:, None, None, None]
    active = gelu_value(mixed).astype(jnp.bfloat16).reshape(slab_shape)
    act_cells = to_cells(active)
    out_cells = vol_cells.astype(jnp.float32) + jnp.dot(
        full_out, act_cells, preferred_element_type=jnp.float32
    )
    block_out = to_channels(out_cells.astype(jnp.bfloat16), slab_shape)
    grad_cells = to_cells(out_grad)
    act_part = lax.dot_general(
        full_out, grad_cells, contract_first, preferred_element_type=jnp.float32
    )
    act_grad = to_channels(act_part.astype(jnp.bfloat16), slab_shape)
    slope = gelu_slope(mixed)
    mix_grad = (
        (act_grad.astype(jnp.float32).reshape(slope.shape) * slope)
        .astype(jnp.bfloat16)
        .reshape(slab_shape)
    )
    padded_grad = lift(with_halo(mix_grad, (("space", 1),), 1))
    hid_grad = core(padded_grad, filter_taps, -1).astype(jnp.bfloat16).reshape(slab_shape)
    hid_cells = to_cells(hid_grad)
    back_part = lax.dot_general(
        full_in, hid_cells, contract_first, preferred_element_type=jnp.float32
    )
    volume_grad = to_channels(
        (grad_cells.astype(jnp.float32) + back_part).astype(jnp.bfloat16), slab_shape
    )
    return (block_out, volume_grad)


def solution(mesh):
    placed = (
        P(("groups", "chan"), "space", None),
        P(("groups", "chan"), "space", None),
        P("chan", None),
        P("chan", None),
        P("chan", None),
        P("chan"),
    )
    return jax.shard_map(
        body,
        mesh=mesh,
        in_specs=placed,
        out_specs=(P(("groups", "chan"), "space", None), P(("groups", "chan"), "space", None)),
        check_vma=False,
    )
```

profile of v0, /device:TPU:0, one launch (start us, length us, event | category | flops | bytes accessed | tf_op | source)
XLA Modules:
  0.0 338.9 jit_solution(1226160043802990815)
XLA Ops:
  7.2 0.0 all-gather.3.cloned.1.call-start
  7.2 0.7 all-gather.3.cloned.1.call-update
  7.9 0.0 copy-start.2
  7.9 2.5 copy.26
  10.4 6.3 %all-to-all-start = ((bf16[256,4,512]{2,0,1:T(8,128)(2,1)}), bf16[256,4,512]{2,0,1:T(8,128)(2,1)S(1)}, u32[]{:S(2)}, u32[]{:S(2)}) async-start(bf16[256,4,512]{2,0,1:T(8,128)(2,1)} %copy.26), calls=%async_computation | async-start | bytes 2097152 | tf_op jit(solution)/shard_map/all_to_all | solution.py:66
  16.7 0.0 all-gather.5.cloned.1.call-start
  16.7 0.7 all-gather.5.cloned.1.call-update
  17.4 0.0 copy-done.2
  17.5 1.2 copy.31
  18.6 49.2 %all-to-all-done = bf16[256,4,512]{2,0,1:T(8,128)(2,1)S(1)} async-done(((bf16[256,4,512]{2,0,1:T(8,128)(2,1)}), bf16[256,4,512]{2,0,1:T(8,128)(2,1)S(1)}, u32[]{:S(2)}, u32[]{:S(2)}) %all-to-all-start) | async-done | bytes 1048608 | tf_op jit(solution)/shard_map/all_to_all | solution.py:66
  67.8 0.0 copy-start
  67.8 3.5 %all-to-all-start.4 = ((bf16[256,4,512]{2,0,1:T(8,128)(2,1)}), bf16[256,4,512]{2,0,1:T(8,128)(2,1)S(1)}, u32[]{:S(2)}, u32[]{:S(2)}) async-start(bf16[256,4,512]{2,0,1:T(8,128)(2,1)} %copy.31), calls=%async_computation.4 | async-start | bytes 2097152 | tf_op jit(solution)/shard_map/all_to_all | solution.py:66
  71.3 15.9 %all-gather.3.cloned.1.call-done = bf16[1024,1024]{1,0:T(8,128)(2,1)} async-done(((bf16[256,1024]{1,0:T(8,128)(2,1)}), bf16[1024,1024]{1,0:T(8,128)(2,1)}) %all-gather.3.cloned.1.call-update) | async-done | bytes 2097168 | tf_op jit(solution)/shard_map/all_gather | solution.py:81
  87.2 2.8 convolution_convert_fusion.1
  90.1 0.0 copy-done
  90.1 1.3 copy.28
  91.4 7.3 %all-to-all-done.4 = bf16[256,4,512]{2,0,1:T(8,128)(2,1)S(1)} async-done(((bf16[256,4,512]{2,0,1:T(8,128)(2,1)}), bf16[256,4,512]{2,0,1:T(8,128)(2,1)S(1)}, u32[]{:S(2)}, u32[]{:S(2)}) %all-to-all-start.4) | async-done | bytes 1048608 | tf_op jit(solution)/shard_map/all_to_all | solution.py:66
  98.7 3.5 %all-to-all-start.1 = ((bf16[4,256,512]{1,2,0:T(8,128)(2,1)}), bf16[4,256,512]{1,2,0:T(8,128)(2,1)S(1)}, u32[]{:S(2)}, u32[]{:S(2)}) async-start(bf16[4,256,512]{1,2,0:T(8,128)(2,1)} %copy.28), calls=%async_computation.1 | async-start | bytes 2097152 | tf_op jit(solution)/shard_map/all_to_all | solution.py:72
  102.3 58.5 %all-gather.5.cloned.1.call-done = bf16[1024,1024]{1,0:T(8,128)(2,1)} async-done(((bf16[256,1024]{1,0:T(8,128)(2,1)}), bf16[1024,1024]{1,0:T(8,128)(2,1)}) %all-gather.5.cloned.1.call-update) | async-done | bytes 2097168 | tf_op jit(solution)/shard_map/all_gather | solution.py:82
  160.8 2.9 convolution_convert_fusion
  163.6 1.3 copy.33
  164.9 0.0 all-to-all-done.1
  164.9 3.6 %all-to-all-start.5 = ((bf16[4,256,512]{1,2,0:T(8,128)(2,1)}), bf16[4,256,512]{1,2,0:T(8,128)(2,1)S(1)}, u32[]{:S(2)}, u32[]{:S(2)}) async-start(bf16[4,256,512]{1,2,0:T(8,128)(2,1)} %copy.33), calls=%async_computation.5 | async-start | bytes 2097152 | tf_op jit(solution)/shard_map/all_to_all | solution.py:72
  168.6 0.8 fusion.112
  169.4 1.7 collective-permute-start
  171.2 1.3 collective-permute-start.1
  172.5 0.0 copy-done.4
  172.5 22.0 %all-to-all-done.5 = bf16[4,256,512]{1,2,0:T(8,128)(2,1)S(1)} async-done(((bf16[4,256,512]{1,2,0:T(8,128)(2,1)}), bf16[4,256,512]{1,2,0:T(8,128)(2,1)S(1)}, u32[]{:S(2)}, u32[]{:S(2)}) %all-to-all-start.5) | async-done | bytes 1048608 | tf_op jit(solution)/shard_map/all_to_all | solution.py:72
  194.5 0.2 convert_element_type.63
  194.7 0.0 collective-permute-done
  194.7 0.0 collective-permute-done.1
  194.7 0.0 copy-start.5
  194.8 1.2 maximum_convert_fusion
  196.0 0.0 copy-done.5
  196.0 10.0 %fusion.5 = (bf16[256,4,16,32]{0,3,2,1:T(8,128)(2,1)S(1)}, f32[256,4,16,32]{0,3,2,1:T(8,128)S(1)}) fusion(f32[256,4,16,32]{0,3,2,1:T(8,128)S(1)} %bitcast.72, f32[256]{0:T(256)S(1)} %copy-done.5, f32[256]{0:T(256)S(1)} %bitcast.102, f32[256]{0:T(256)S(1)} %bitcast.104, f32[256]{0:T(256)S(1)} %bitcast.108, f32[256]{0:T(256)S(1)} %bitcast.110, ...), kind=kLoop, calls=%fused_computation.54 | loop fusion | flops 33554432 | bytes 14708736 | tf_op jit(solution)/shard_map/convert_element_type | solution.py:105
  206.0 0.8 fusion.111
  206.9 1.3 collective-permute-start.2
  208.2 1.3 collective-permute-start.3
  209.5 1.4 multiply_convert_fusion
  210.8 3.5 %all-to-all-start.2 = ((bf16[256,4,512]{0,2,1:T(8,128)(2,1)}), bf16[256,4,512]{0,2,1:T(8,128)(2,1)S(1)}, u32[]{:S(2)}, u32[]{:S(2)}) async-start(bf16[256,4,512]{0,2,1:T(8,128)(2,1)} %bitcast.35), calls=%async_computation.2 | async-start | bytes 2097152 | tf_op jit(solution)/shard_map/all_to_all | solution.py:66
  214.3 0.0 collective-permute-done.2
  214.4 0.0 collective-permute-done.3
  214.4 1.2 maximum_convert_fusion.1
  215.6 10.0 %fusion.104 = bf16[256,4,16,32]{0,3,2,1:T(8,128)(2,1)} fusion(f32[256,6,16,32]{0,3,2,1:T(8,128)S(1)} %maximum_convert_fusion.1, f32[256]{0:T(256)S(1)} %bitcast.103, f32[256]{0:T(256)S(1)} %bitcast.105, f32[256]{0:T(256)S(1)} %bitcast.109, f32[256]{0:T(256)S(1)} %bitcast.111, f32[256]{0:T(256)S(1)} %bitcast.113, f32[256]{0:T(256)S(1)} %bitcast.115, ...), kind=kLoop, calls=%fused_computation.153 | loop fusion | flops 28311552 | bytes 10513408 | tf_op jit(solution)/shard_map/convert_element_type | solution.py:109
  225.6 14.8 %all-to-all-done.2 = bf16[256,4,512]{0,2,1:T(8,128)(2,1)S(1)} async-done(((bf16[256,4,512]{0,2,1:T(8,128)(2,1)}), bf16[256,4,512]{0,2,1:T(8,128)(2,1)S(1)}, u32[]{:S(2)}, u32[]{:S(2)}) %all-to-all-start.2) | async-done | bytes 1048608 | tf_op jit(solution)/shard_map/all_to_all | solution.py:66
  240.4 4.3 %all-to-all-start.6 = ((bf16[256,4,512]{0,2,1:T(8,128)(2,1)}), bf16[256,4,512]{0,2,1:T(8,128)(2,1)}, u32[]{:S(2)}, u32[]{:S(2)}) async-start(bf16[256,4,512]{0,2,1:T(8,128)(2,1)} %bitcast.83), calls=%async_computation.6 | async-start | bytes 2097152 | tf_op jit(solution)/shard_map/all_to_all | solution.py:66
  244.7 0.0 copy-done.1
  244.7 1.3 copy.38
  246.0 0.0 copy-start.3
  246.0 1.3 copy.29
  247.3 0.0 copy-done.3
  247.3 3.2 fusion.109
  250.5 1.3 copy.39
  251.8 19.9 %all-to-all-done.6 = bf16[256,4,512]{0,2,1:T(8,128)(2,1)} async-done(((bf16[256,4,512]{0,2,1:T(8,128)(2,1)}), bf16[256,4,512]{0,2,1:T(8,128)(2,1)}, u32[]{:S(2)}, u32[]{:S(2)}) %all-to-all-start.6) | async-done | bytes 1048608 | tf_op jit(solution)/shard_map/all_to_all | solution.py:66
  271.8 3.7 %all-to-all-start.3 = ((bf16[4,256,512]{2,1,0:T(8,128)(2,1)}), bf16[4,256,512]{2,1,0:T(8,128)(2,1)S(1)}, u32[]{:S(2)}, u32[]{:S(2)}) async-start(bf16[4,256,512]{2,1,0:T(8,128)(2,1)} %bitcast.39), calls=%async_computation.3 | async-start | bytes 2097152 | tf_op jit(solution)/shard_map/all_to_all | solution.py:72
  275.5 0.5 copy.40
  276.0 1.5 copy.34
  277.5 3.8 %fusion.108 = bf16[1024,512]{0,1:T(8,128)(2,1)} fusion(bf16[1024,512]{0,1:T(8,128)(2,1)S(1)} %copy.40, bf16[1024,512]{1,0:T(8,128)(2,1)S(1)} %bitcast.85, bf16[1024,1024]{1,0:T(8,128)(2,1)} %all-gather.3.cloned.1.call-done), kind=kOutput, calls=%fused_computation.164 | convolution fusion | flops 1075314688 | bytes 5242880 | tf_op jit(solution)/shard_map/dot_general | solution.py:111
  281.4 2.3 copy.41
  283.6 17.8 %all-to-all-done.3 = bf16[4,256,512]{2,1,0:T(8,128)(2,1)S(1)} async-done(((bf16[4,256,512]{2,1,0:T(8,128)(2,1)}), bf16[4,256,512]{2,1,0:T(8,128)(2,1)S(1)}, u32[]{:S(2)}, u32[]{:S(2)}) %all-to-all-start.3) | async-done | bytes 1048608 | tf_op jit(solution)/shard_map/all_to_all | solution.py:72
  301.5 3.5 %all-to-all-start.7 = ((bf16[4,256,512]{2,1,0:T(8,128)(2,1)}), bf16[4,256,512]{2,1,0:T(8,128)(2,1)S(1)}, u32[]{:S(2)}, u32[]{:S(2)}) async-start(bf16[4,256,512]{2,1,0:T(8,128)(2,1)} %bitcast.54), calls=%async_computation.7 | async-start | bytes 2097152 | tf_op jit(solution)/shard_map/all_to_all | solution.py:72
  305.0 1.8 copy.36
  306.8 23.6 %all-to-all-done.7 = bf16[4,256,512]{2,1,0:T(8,128)(2,1)S(1)} async-done(((bf16[4,256,512]{2,1,0:T(8,128)(2,1)}), bf16[4,256,512]{2,1,0:T(8,128)(2,1)S(1)}, u32[]{:S(2)}, u32[]{:S(2)}) %all-to-all-start.7) | async-done | bytes 1048608 | tf_op jit(solution)/shard_map/all_to_all | solution.py:72
  330.3 1.8 copy.37
  (4 shorter events, 0.0 us)
Async XLA Ops:
  7.2 80.1 %all-gather.3.cloned.1.call-start = ((), (), s32[]{:S(2)}) async-start(), calls=%async_computation.8 | async-start | bytes 2621440 | tf_op jit(solution)/shard_map/all_gather | solution.py:81
  7.9 9.5 %copy-start.2 = (bf16[256,4,512]{2,1,0:T(4,128)(2,1)S(1)}, bf16[256,4,512]{2,1,0:T(4,128)(2,1)}, u32[]{:S(2)}) copy-start(bf16[256,4,512]{2,1,0:T(4,128)(2,1)} %param.7) | copy-start | bytes 3145732
  10.4 57.4 %all-to-all-start = ((bf16[256,4,512]{2,0,1:T(8,128)(2,1)}), bf16[256,4,512]{2,0,1:T(8,128)(2,1)S(1)}, u32[]{:S(2)}, u32[]{:S(2)}) async-start(bf16[256,4,512]{2,0,1:T(8,128)(2,1)} %copy.26), calls=%async_computation | async-start | bytes 2097152 | tf_op jit(solution)/shard_map/all_to_all | solution.py:66
  16.7 144.0 %all-gather.5.cloned.1.call-start = ((), (), s32[]{:S(2)}) async-start(), calls=%async_computation.9 | async-start | bytes 2621440 | tf_op jit(solution)/shard_map/all_gather | solution.py:82
  67.8 22.3 %copy-start = (bf16[256,4,512]{2,0,1:T(8,128)(2,1)}, bf16[256,4,512]{2,0,1:T(8,128)(2,1)S(1)}, u32[]{:S(2)}) copy-start(bf16[256,4,512]{2,0,1:T(8,128)(2,1)S(1)} %all-to-all-done) | copy-start | bytes 3145732
  67.8 30.9 %all-to-all-start.4 = ((bf16[256,4,512]{2,0,1:T(8,128)(2,1)}), bf16[256,4,512]{2,0,1:T(8,128)(2,1)S(1)}, u32[]{:S(2)}, u32[]{:S(2)}) async-start(bf16[256,4,512]{2,0,1:T(8,128)(2,1)} %copy.31), calls=%async_computation.4 | async-start | bytes 2097152 | tf_op jit(solution)/shard_map/all_to_all | solution.py:66
  98.7 66.2 %all-to-all-start.1 = ((bf16[4,256,512]{1,2,0:T(8,128)(2,1)}), bf16[4,256,512]{1,2,0:T(8,128)(2,1)S(1)}, u32[]{:S(2)}, u32[]{:S(2)}) async-start(bf16[4,256,512]{1,2,0:T(8,128)(2,1)} %copy.28), calls=%async_computation.1 | async-start | bytes 2097152 | tf_op jit(solution)/shard_map/all_to_all | solution.py:72
  164.9 7.5 %copy-start.4 = (f32[256,27]{0,1:T(8,128)S(1)}, f32[256,27]{0,1:T(8,128)}, u32[]{:S(2)}) copy-start(f32[256,27]{0,1:T(8,128)} %param.10) | copy-start | bytes 82948
  164.9 29.6 %all-to-all-start.5 = ((bf16[4,256,512]{1,2,0:T(8,128)(2,1)}), bf16[4,256,512]{1,2,0:T(8,128)(2,1)S(1)}, u32[]{:S(2)}, u32[]{:S(2)}) async-start(bf16[4,256,512]{1,2,0:T(8,128)(2,1)} %copy.33), calls=%async_computation.5 | async-start | bytes 2097152 | tf_op jit(solution)/shard_map/all_to_all | solution.py:72
  169.4 25.3 %collective-permute-start = (bf16[256,1,512]{0,2,1:T(8,128)(2,1)}, bf16[256,1,512]{0,2,1:T(8,128)(2,1)S(1)}, u32[]{:S(2)}, u32[]{:S(2)}) collective-permute-start(bf16[256,1,512]{0,2,1:T(8,128)(2,1)} %get-tuple-element.8), channel_id=1, source_target_pairs={{0,1},{1,2},{2,3},{4,5},{5,6},{6,7},{8,9},{9,10},{10,11},{12,13},{... | collective-permute-start | bytes 786440 | tf_op jit(solution)/shard_map/ppermute | solution.py:19
  171.2 23.6 %collective-permute-start.1 = (bf16[256,1,512]{0,2,1:T(8,128)(2,1)}, bf16[256,1,512]{0,2,1:T(8,128)(2,1)}, u32[]{:S(2)}, u32[]{:S(2)}) collective-permute-start(bf16[256,1,512]{0,2,1:T(8,128)(2,1)} %get-tuple-element.9), channel_id=1, source_target_pairs={{1,0},{2,1},{3,2},{5,4},{6,5},{7,6},{9,8},{10,9},{11,10},{13,12},{... | collective-permute-start | bytes 786440 | tf_op jit(solution)/shard_map/ppermute | solution.py:22
  194.7 1.2 copy-start.5
  206.9 7.5 %collective-permute-start.2 = (bf16[256,1,512]{0,2,1:T(8,128)(2,1)}, bf16[256,1,512]{0,2,1:T(8,128)(2,1)S(1)}, u32[]{:S(2)}, u32[]{:S(2)}) collective-permute-start(bf16[256,1,512]{0,2,1:T(8,128)(2,1)} %get-tuple-element.6), channel_id=1, source_target_pairs={{0,1},{1,2},{2,3},{4,5},{5,6},{6,7},{8,9},{9,10},{10,11},{12,13},{... | collective-permute-start | bytes 786440 | tf_op jit(solution)/shard_map/ppermute | solution.py:19
  208.2 6.2 %collective-permute-start.3 = (bf16[256,1,512]{0,2,1:T(8,128)(2,1)}, bf16[256,1,512]{0,2,1:T(8,128)(2,1)}, u32[]{:S(2)}, u32[]{:S(2)}) collective-permute-start(bf16[256,1,512]{0,2,1:T(8,128)(2,1)} %get-tuple-element.7), channel_id=1, source_target_pairs={{1,0},{2,1},{3,2},{5,4},{6,5},{7,6},{9,8},{10,9},{11,10},{13,12},{... | collective-permute-start | bytes 786440 | tf_op jit(solution)/shard_map/ppermute | solution.py:22
  210.8 29.6 %all-to-all-start.2 = ((bf16[256,4,512]{0,2,1:T(8,128)(2,1)}), bf16[256,4,512]{0,2,1:T(8,128)(2,1)S(1)}, u32[]{:S(2)}, u32[]{:S(2)}) async-start(bf16[256,4,512]{0,2,1:T(8,128)(2,1)} %bitcast.35), calls=%async_computation.2 | async-start | bytes 2097152 | tf_op jit(solution)/shard_map/all_to_all | solution.py:66
  225.6 19.0 %copy-start.1 = (bf16[256,4,512]{2,0,1:T(8,128)(2,1)S(1)}, bf16[256,4,512]{2,0,1:T(8,128)(2,1)}, u32[]{:S(2)}) copy-start(bf16[256,4,512]{2,0,1:T(8,128)(2,1)} %copy-done) | copy-start | bytes 3145732
  240.4 31.4 %all-to-all-start.6 = ((bf16[256,4,512]{0,2,1:T(8,128)(2,1)}), bf16[256,4,512]{0,2,1:T(8,128)(2,1)}, u32[]{:S(2)}, u32[]{:S(2)}) async-start(bf16[256,4,512]{0,2,1:T(8,128)(2,1)} %bitcast.83), calls=%async_computation.6 | async-start | bytes 2097152 | tf_op jit(solution)/shard_map/all_to_all | solution.py:66
  246.0 1.3 copy-start.3
  271.8 29.7 %all-to-all-start.3 = ((bf16[4,256,512]{2,1,0:T(8,128)(2,1)}), bf16[4,256,512]{2,1,0:T(8,128)(2,1)S(1)}, u32[]{:S(2)}, u32[]{:S(2)}) async-start(bf16[4,256,512]{2,1,0:T(8,128)(2,1)} %bitcast.39), calls=%async_computation.3 | async-start | bytes 2097152 | tf_op jit(solution)/shard_map/all_to_all | solution.py:72
  301.5 28.9 %all-to-all-start.7 = ((bf16[4,256,512]{2,1,0:T(8,128)(2,1)}), bf16[4,256,512]{2,1,0:T(8,128)(2,1)S(1)}, u32[]{:S(2)}, u32[]{:S(2)}) async-start(bf16[4,256,512]{2,1,0:T(8,128)(2,1)} %bitcast.54), calls=%async_computation.7 | async-start | bytes 2097152 | tf_op jit(solution)/shard_map/all_to_all | solution.py:72
Sparse Core Ops, SparseCore 0:
  9.6 77.6 all-gather.2
  88.8 71.9 all-gather.4
where the time goes:
time: 340 us; the launch traced here: 339 us
  waiting for transfers between devices  230 us (68%)
  starting transfers between devices  37.6 us (11%)
  other arithmetic  24 us (7%)
  local copies, waits for them, and re-layouts  19.9 us (6%)
  between operations  14.3 us (4%)
  matrix products  12.8 us (4%)
    all_to_all x4, waiting for transfers between devices, to_cells(): lax.all_to_all(field.reshape(field.shape[0], -1), 'chan', split_axis=1, c...  91.2 us
    all_to_all x4, waiting for transfers between devices, to_channels(): lax.all_to_all(field, 'chan', split_axis=0, concat_axis=1, tiled=True)  63.4 us
    all_gather x1, waiting for transfers between devices, body(): lax.all_gather(weight_out, 'chan', axis=0, tiled=True)  58.5 us
    all_to_all x4, starting transfers between devices, to_cells(): lax.all_to_all(field.reshape(field.shape[0], -1), 'chan', split_axis=1, c...  17.6 us
    all_gather x1, waiting for transfers between devices, body(): lax.all_gather(weight_in, 'chan', axis=0, tiled=True)  15.9 us
    all_to_all x4, starting transfers between devices, to_channels(): lax.all_to_all(field, 'chan', split_axis=0, concat_axis=1, tiled=True)  14.4 us
    convert_element_type x1, other arithmetic, body(): core(padded_grad, filter_taps, -1).astype(jnp.bfloat16).reshape(slab_shape)  10 us
    convert_element_type x1, other arithmetic, body(): mix_grad = (act_grad.astype(jnp.float32).reshape(slope.shape) * slope).as...  10 us
  transfers between devices with their start and end apart: 14, of which 9 were waited for; matrix products, arithmetic and copies ran while one was open for 13% of the time, Pallas kernels for 0%

commit v1 on v0

--- a/solution.py
+++ b/solution.py
@@ -1,6 +1,10 @@
+import functools
+
 import jax
 import jax.numpy as jnp
 from jax import lax
+from jax.experimental import pallas as pl
+from jax.experimental.pallas import tpu as pltpu
 from jax.sharding import PartitionSpec as P
 
 CX = 32
@@ -74,7 +78,7 @@
     )
 
 
-def body(volume, out_grad, weight_in, weight_out, filter_taps, filter_bias):
+def general_body(volume, out_grad, weight_in, weight_out, filter_taps, filter_bias):
     slab_shape = volume.shape
     contract_first = (((0,), (0,)), ((), ()))
     full_in, full_out = (
@@ -115,6 +119,508 @@
         (grad_cells.astype(jnp.float32) + back_part).astype(jnp.bfloat16), slab_shape
     )
     return (block_out, volume_grad)
+
+
+LANES = 128
+TAP_ROWS = 32
+MESH = pl.DeviceIdType.MESH
+f32 = jnp.float32
+bf16 = jnp.bfloat16
+
+
+def rolled(value, shift):
+    shift = shift % LANES
+    return value if shift == 0 else pltpu.roll(value, shift, 1)
+
+
+def kernel(
+    nc,
+    ns,
+    vol,
+    grd,
+    win,
+    wout,
+    tap,
+    bo,
+    vg,
+    cells,
+    weights,
+    tap_t,
+    tap_s,
+    field,
+    pack_y,
+    halo_y,
+    pack_c,
+    halo_c,
+    active,
+    slope,
+    hid,
+    stage,
+    a_send,
+    a_recv,
+    w1_send,
+    w1_recv,
+    w2_send,
+    w2_recv,
+    t_send,
+    t_recv,
+    h_send,
+    h_recv,
+    own_sem,
+):
+    planes, block, _ = vol.shape
+    channels = block * nc
+    part = block // ns
+    g = lax.axis_index("groups")
+    c = lax.axis_index("chan")
+    s = lax.axis_index("space")
+    grads = (vol, grd)
+    shards = (win, wout)
+    outs = (bo, vg)
+
+    def chan_peer(d):
+        return lax.rem(c + d, nc)
+
+    def space_peer(d):
+        return lax.rem(s + d, ns)
+
+    def rows_of(r):
+        return pl.ds(pl.multiple_of(r * block, block), block)
+
+    def lanes_of(q):
+        return pl.ds(pl.multiple_of(q * LANES, LANES), LANES)
+
+    def part_rows(r, q):
+        return pl.ds(pl.multiple_of(r * block + q * part, part), part)
+
+    def remote(src, dst, send, recv, to):
+        return pltpu.make_async_remote_copy(
+            src_ref=src, dst_ref=dst, send_sem=send, recv_sem=recv, device_id=to, device_id_type=MESH
+        )
+
+    def in_copy(k, frm, to):
+        return remote(
+            grads[k].at[:, :, lanes_of(to)],
+            cells.at[k, :, rows_of(frm), :],
+            a_send.at[k, to],
+            a_recv.at[k, frm],
+            (g, to, s),
+        )
+
+    def out_copy(k, frm, to):
+        return remote(
+            stage.at[k, :, rows_of(to), :],
+            outs[k].at[:, :, lanes_of(frm)],
+            a_send.at[2 + k, to],
+            a_recv.at[2 + k, frm],
+            (g, to, s),
+        )
+
+    def w1_copy(k, frm, to):
+        return remote(
+            shards[k].at[pl.ds(pl.multiple_of(s * part, part), part), :],
+            weights.at[k, part_rows(frm, s), :],
+            w1_send.at[k, to],
+            w1_recv.at[k, frm],
+            (g, to, s),
+        )
+
+    def w2_copy(k, shard, frm, to):
+        return remote(
+            weights.at[k, part_rows(shard, frm), :],
+            weights.at[k, part_rows(shard, frm), :],
+            w2_send.at[k, shard, to],
+            w2_recv.at[k, shard, frm],
+            (g, c, to),
+        )
+
+    def tap_copy(frm, to):
+        return remote(tap, tap_t.at[frm], t_send.at[to], t_recv.at[frm], (g, to, s))
+
+    def halo_copy(v, way, r):
+        rw = rows_of(r)
+        if way == 0:
+            src, dst, to = pack_y.at[v, 0, rw, :], halo_y.at[v, 0, rw, :], (g, c + 1, s)
+        elif way == 1:
+            src, dst, to = pack_y.at[v, 1, rw, :], halo_y.at[v, 1, rw, :], (g, c - 1, s)
+        elif way == 2:
+            src, dst, to = field.at[v, planes, rw, :], field.at[v, 0, rw, :], (g, c, s + 1)
+        elif way == 3:
+            src, dst, to = field.at[v, 1, rw, :], field.at[v, planes + 1, rw, :], (g, c, s - 1)
+        elif way == 4:
+            src, dst, to = pack_c.at[v, 0, rw, :], halo_c.at[v, 0, rw, :], (g, c, s + 1)
+        else:
+            src, dst, to = pack_c.at[v, 1, rw, :], halo_c.at[v, 1, rw, :], (g, c, s - 1)
+        return remote(src, dst, h_send.at[v, way, r], h_recv.at[v, way, r], to)
+
+    sends_when = (c < nc - 1, c > 0, s < ns - 1, s > 0, s < ns - 1, s > 0)
+    takes_when = (c > 0, c < nc - 1, s > 0, s < ns - 1, s > 0, s < ns - 1)
+
+    def halo_start(v, ways, r):
+        for way in ways:
+            pl.when(sends_when[way])(lambda way=way: halo_copy(v, way, r).start())
+
+    def halo_wait_recv(v, ways, r):
+        for way in ways:
+            pl.when(takes_when[way])(lambda way=way: halo_copy(v, way, r).wait_recv())
+
+    def halo_wait_send(v, ways, r):
+        for way in ways:
+            pl.when(sends_when[way])(lambda way=way: halo_copy(v, way, r).wait_send())
+
+    barrier = pltpu.get_barrier_semaphore()
+    for d in range(1, nc):
+        pl.semaphore_signal(barrier, inc=1, device_id=(g, chan_peer(d), s), device_id_type=MESH)
+    for d in range(1, ns):
+        pl.semaphore_signal(barrier, inc=1, device_id=(g, c, space_peer(d)), device_id_type=MESH)
+    pl.semaphore_wait(barrier, nc + ns - 2)
+
+    own = []
+    for k in range(2):
+        own.append(
+            pltpu.make_async_copy(
+                grads[k].at[:, :, lanes_of(c)], cells.at[k, :, rows_of(c), :], own_sem.at[2 * k]
+            )
+        )
+        own.append(
+            pltpu.make_async_copy(shards[k], weights.at[k, rows_of(c), :], own_sem.at[2 * k + 1])
+        )
+
+    for d in range(1, nc):
+        w1_copy(0, c, chan_peer(d)).start()
+    for d in range(1, nc):
+        tap_copy(c, chan_peer(d)).start()
+    for d in range(1, nc):
+        in_copy(0, c, chan_peer(d)).start()
+    for d in range(1, nc):
+        w1_copy(1, c, chan_peer(d)).start()
+    for d in range(1, nc):
+        in_copy(1, c, chan_peer(d)).start()
+    for copy in own:
+        copy.start()
+
+    zeros = jnp.zeros((channels, LANES), bf16)
+    for v in range(2):
+
+        @pl.when(c == 0)
+        def _():
+            halo_y[v, 0] = zeros
+
+        @pl.when(c == nc - 1)
+        def _():
+            halo_y[v, 1] = zeros
+
+        @pl.when(s == 0)
+        def _():
+            field[v, 0] = zeros
+            halo_c[v, 0] = zeros
+
+        @pl.when(s == ns - 1)
+        def _():
+            field[v, planes + 1] = zeros
+            halo_c[v, 1] = zeros
+
+    tap_t[c] = tap[...]
+
+    def spread(k):
+        for d in range(1, nc):
+            p = chan_peer(d)
+            w1_copy(k, p, c).wait_recv()
+            for e in range(1, ns):
+                w2_copy(k, p, s, space_peer(e)).start()
+
+    def await_weights(k):
+        for d in range(1, nc):
+            p = chan_peer(d)
+            for e in range(1, ns):
+                w2_copy(k, p, space_peer(e), s).wait_recv()
+
+    spread(0)
+    for d in range(1, nc):
+        tap_copy(chan_peer(d), c).wait_recv()
+    for r in range(nc):
+        tap_s[r * block : (r + 1) * block, 0:TAP_ROWS] = jnp.transpose(tap_t[r])
+    for copy in own:
+        copy.wait()
+    for d in range(1, nc):
+        in_copy(0, chan_peer(d), c).wait_recv()
+    await_weights(0)
+
+    def wide(ref, first, rw):
+        return jnp.concatenate([ref[first + (z,) + (rw, slice(None))] for z in range(planes)], axis=1)
+
+    every = slice(None)
+
+    def pack(v, r):
+        step = 32
+
+        def one(i, carry):
+            rw = pl.ds(pl.multiple_of(r * block + i * step, step), step)
+            spot = lax.broadcasted_iota(jnp.int32, (step, LANES), 1)
+            values = [field[v, 1 + z, rw, :].astype(f32) for z in range(planes)]
+            high, low = values[planes - 1], values[0]
+            high = rolled(values[planes - 1], CX * planes)
+            for z in range(planes):
+                here = (spot >= z * CX) & (spot < (z + 1) * CX)
+                high = jnp.where(here, rolled(values[z], CX * (z + 1)), high)
+                low = jnp.where(here, rolled(values[z], CX * z), low)
+            pack_y[v, 0, rw, :] = high.astype(bf16)
+            pack_y[v, 1, rw, :] = low.astype(bf16)
+            return carry
+
+        lax.fori_loop(0, block // step, one, 0)
+
+    def corner(v, r):
+        step = 32
+
+        def one(i, carry):
+            rw = pl.ds(pl.multiple_of(r * block + i * step, step), step)
+            spot = lax.broadcasted_iota(jnp.int32, (step, LANES), 1)
+            low = halo_y[v, 0, rw, :].astype(f32)
+            high = halo_y[v, 1, rw, :].astype(f32)
+            last = LANES - CX
+            first = spot < CX
+            z = planes - 1
+            pack_c[v, 0, rw, :] = jnp.where(first, rolled(low, -CX * z), rolled(high, last - CX * z)).astype(bf16)
+            pack_c[v, 1, rw, :] = jnp.where(first, low, rolled(high, last)).astype(bf16)
+            return carry
+
+        lax.fori_loop(0, block // step, one, 0)
+
+    def convolve(v, r, finish):
+        step = 16
+        half = 8
+
+        def one(i, carry):
+            rw = pl.ds(pl.multiple_of(r * block + i * step, step), step)
+            spot = lax.broadcasted_iota(jnp.int32, (half, LANES), 1)
+            column = lax.rem(spot, CX)
+            first = spot < CX
+            final = spot >= LANES - CX
+            loaded = [field[v, z, rw, :].astype(f32) for z in range(planes + 2)]
+            low = halo_y[v, 0, rw, :].astype(f32)
+            high = halo_y[v, 1, rw, :].astype(f32)
+            below = halo_c[v, 0, rw, :].astype(f32)
+            above = halo_c[v, 1, rw, :].astype(f32)
+            taps = tap_s[rw, :]
+            results = [[] for _ in range(planes)]
+            for q in range(step // half):
+                cut = slice(q * half, (q + 1) * half)
+                shifted = []
+                for z in range(planes + 2):
+                    value = loaded[z][cut]
+                    if z == 0:
+                        under = over = below[cut]
+                    elif z == planes + 1:
+                        under = over = above[cut]
+                    else:
+                        under = rolled(low[cut], -CX * (z - 1))
+                        over = rolled(high[cut], LANES - CX - CX * (z - 1))
+                    shifted.append(
+                        (
+                            jnp.where(first, under, rolled(value, CX)),
+                            value,
+                            jnp.where(final, over, rolled(value, -CX)),
+                        )
+                    )
+                weight = []
+                for k in range(27):
+                    at = k if v == 0 else 26 - k
+                    weight.append(jnp.broadcast_to(taps[cut, at : at + 1], (half, LANES)))
+                bias = jnp.broadcast_to(taps[cut, 27:28], (half, LANES)) if v == 0 else None
+                for z in range(planes):
+                    sums = [None, None, None]
+                    for a in range(3):
+                        for b in range(3):
+                            for e in range(3):
+                                term = weight[9 * a + 3 * b + e] * shifted[z + a][b]
+                                sums[e] = term if sums[e] is None else sums[e] + term
+                    total = sums[1]
+                    total = total + jnp.where(column == 0, 0.0, rolled(sums[0], 1))
+                    total = total + jnp.where(column == CX - 1, 0.0, rolled(sums[2], -1))
+                    if bias is not None:
+                        total = total + bias
+                    results[z].append(total)
+            for z in range(planes):
+                finish(z, rw, jnp.concatenate(results[z], axis=0))
+            return carry
+
+        lax.fori_loop(0, block // step, one, 0)
+
+    def finish_forward(z, rw, mixed):
+        up = 0.5 * (1.0 + lax.erf(mixed * root_half))
+        active[z, rw, :] = (mixed * up).astype(bf16)
+        slope[z, rw, :] = up + mixed * jnp.exp(-0.5 * mixed * mixed) * inv_root_two_pi
+
+    def finish_backward(z, rw, total):
+        hid[z, rw, :] = total.astype(bf16)
+
+    def hidden_chunk(r, carry):
+        rw = rows_of(r)
+        value = jnp.dot(weights[0, rw, :], wide(cells, (0,), every), preferred_element_type=f32)
+        for z in range(planes):
+            field[0, 1 + z, rw, :] = value[:, z * LANES : (z + 1) * LANES].astype(bf16)
+        halo_start(0, (2, 3), r)
+        pack(0, r)
+        halo_start(0, (0, 1), r)
+        return carry
+
+    def corner_chunk(v):
+        def run(r, carry):
+            halo_wait_recv(v, (0, 1), r)
+            corner(v, r)
+            halo_start(v, (4, 5), r)
+            return carry
+
+        lax.fori_loop(0, nc, run, 0)
+
+    def conv_chunk(v, finish):
+        def run(r, carry):
+            halo_wait_recv(v, (2, 3, 4, 5), r)
+            convolve(v, r, finish)
+            return carry
+
+        lax.fori_loop(0, nc, run, 0)
+
+    def out_chunk(k, r, value):
+        total = wide(cells, (k,), rows_of(r)).astype(f32) + value
+        for z in range(planes):
+            stage[k, z, rows_of(r), :] = total[:, z * LANES : (z + 1) * LANES].astype(bf16)
+
+        @pl.when(r != c)
+        def _():
+            out_copy(k, c, r).start()
+
+        @pl.when(r == c)
+        def _():
+            outs[k][:, :, lanes_of(c)] = stage[k, :, rows_of(r), :]
+
+    def block_chunk(r, carry):
+        value = jnp.dot(weights[1, rows_of(r), :], wide(active, (), every), preferred_element_type=f32)
+        out_chunk(0, r, value)
+        return carry
+
+    def flipped(k, r, right):
+        return lax.dot_general(
+            weights[k, :, rows_of(r)], right, (((0,), (0,)), ((), ())), preferred_element_type=f32
+        )
+
+    def mix_chunk(r, carry):
+        rw = rows_of(r)
+        value = flipped(1, r, wide(cells, (1,), every))
+        for z in range(planes):
+            act = value[:, z * LANES : (z + 1) * LANES].astype(bf16).astype(f32)
+            field[1, 1 + z, rw, :] = (act * slope[z, rw, :]).astype(bf16)
+        halo_start(1, (2, 3), r)
+        pack(1, r)
+        halo_start(1, (0, 1), r)
+        return carry
+
+    def back_chunk(r, carry):
+        out_chunk(1, r, flipped(0, r, wide(hid, (), every)))
+        return carry
+
+    lax.fori_loop(0, nc, hidden_chunk, 0)
+    spread(1)
+    corner_chunk(0)
+    conv_chunk(0, finish_forward)
+    await_weights(1)
+    lax.fori_loop(0, nc, block_chunk, 0)
+    for d in range(1, nc):
+        in_copy(1, chan_peer(d), c).wait_recv()
+    lax.fori_loop(0, nc, mix_chunk, 0)
+    corner_chunk(1)
+    conv_chunk(1, finish_backward)
+    lax.fori_loop(0, nc, back_chunk, 0)
+
+    for d in range(1, nc):
+        p = chan_peer(d)
+        tap_copy(c, p).wait_send()
+        for k in range(2):
+            w1_copy(k, c, p).wait_send()
+            in_copy(k, c, p).wait_send()
+            for e in range(1, ns):
+                w2_copy(k, p, s, space_peer(e)).wait_send()
+
+    def drain(r, carry):
+        for v in range(2):
+            halo_wait_send(v, range(6), r)
+        return carry
+
+    lax.fori_loop(0, nc, drain, 0)
+    for d in range(1, nc):
+        p = chan_peer(d)
+        for k in range(2):
+            out_copy(k, c, p).wait_send()
+            out_copy(k, p, c).wait_recv()
+
+
+def body(mesh, volume, out_grad, weight_in, weight_out, filter_taps, filter_bias):
+    nc, ns = mesh.shape["chan"], mesh.shape["space"]
+    block, planes, plane = volume.shape
+    channels = weight_in.shape[1]
+    fits = (
+        nc > 1
+        and ns > 1
+        and plane == nc * LANES
+        and plane == CX * CY
+        and planes * CX == LANES
+        and block * nc == channels
+        and block % (ns * 16) == 0
+        and block % LANES == 0
+    )
+    if not fits:
+        return general_body(volume, out_grad, weight_in, weight_out, filter_taps, filter_bias)
+    spare = jnp.zeros((TAP_ROWS - filter_taps.shape[1] - 1, block), f32)
+    tap = jnp.concatenate([filter_taps.T, filter_bias[None, :], spare], axis=0)
+    shape = jax.ShapeDtypeStruct((planes, block, plane), bf16)
+    vmem = pl.BlockSpec(memory_space=pltpu.VMEM)
+    dma = pltpu.SemaphoreType.DMA
+    block_out, volume_grad = pl.pallas_call(
+        functools.partial(kernel, nc, ns),
+        out_shape=(shape, shape),
+        in_specs=[vmem] * 5,
+        out_specs=(vmem, vmem),
+        scratch_shapes=[
+            pltpu.VMEM((2, planes, channels, LANES), bf16),
+            pltpu.VMEM((2, channels, channels), bf16),
+            pltpu.VMEM((nc, TAP_ROWS, block), f32),
+            pltpu.VMEM((channels, LANES), f32),
+            pltpu.VMEM((2, planes + 2, channels, LANES), bf16),
+            pltpu.VMEM((2, 2, channels, LANES), bf16),
+            pltpu.VMEM((2, 2, channels, LANES), bf16),
+            pltpu.VMEM((2, 2, channels, LANES), bf16),
+            pltpu.VMEM((2, 2, channels, LANES), bf16),
+            pltpu.VMEM((planes, channels, LANES), bf16),
+            pltpu.VMEM((planes, channels, LANES), f32),
+            pltpu.VMEM((planes, channels, LANES), bf16),
+            pltpu.VMEM((2, planes, channels, LANES), bf16),
+            dma((4, nc)),
+            dma((4, nc)),
+            dma((2, nc)),
+            dma((2, nc)),
+            dma((2, nc, ns)),
+            dma((2, nc, ns)),
+            dma((nc,)),
+            dma((nc,)),
+            dma((2, 6, nc)),
+            dma((2, 6, nc)),
+            dma((4,)),
+        ],
+        compiler_params=pltpu.CompilerParams(
+            collective_id=0, has_side_effects=True, vmem_limit_bytes=56 * 1024 * 1024
+        ),
+        cost_estimate=pl.CostEstimate(
+            flops=8 * channels * channels * plane, bytes_accessed=12 * block * plane * planes, transcendentals=0
+        ),
+    )(
+        jnp.transpose(volume, (1, 0, 2)),
+        jnp.transpose(out_grad, (1, 0, 2)),
+        weight_in,
+        weight_out,
+        tap,
+    )
+    return jnp.transpose(block_out, (1, 0, 2)), jnp.transpose(volume_grad, (1, 0, 2))
 
 
 def solution(mesh):
@@ -127,7 +633,7 @@
         P("chan"),
     )
     return jax.shard_map(
-        body,
+        functools.partial(body, mesh),
         mesh=mesh,
         in_specs=placed,
         out_specs=(P(("groups", "chan"), "space", None), P(("groups", "chan"), "space", None)),

time: 340 us -> 185 us (0.54)
  waiting for transfers between devices: 230 us -> 0 us
  Pallas kernels: 0 us -> 171 us
  starting transfers between devices: 37.6 us -> 0 us
  other arithmetic: 24 us -> 1.43 us
  between operations: 14.3 us -> 0.66 us
  matrix products: 12.8 us -> 0 us
  local copies, waits for them, and re-layouts: 19.9 us -> 8.83 us
    pallas_call x0 -> x1, Pallas kernels: none -> 171 us  [body(): pl.pallas_call(functools.partial(kernel, nc, ns), out_shape=(shape, shape...]
    all_to_all x8 -> x0, waiting for transfers between devices: 155 us -> none  [the longest x4 91.2 us: to_cells(): lax.all_to_all(field.reshape(field.shape[0], -1), 'chan', split_axis=1, c...]
    all_gather x2 -> x0, waiting for transfers between devices: 74.4 us -> none  [the longest x1 58.5 us: body(): lax.all_gather(weight_out, 'chan', axis=0, tiled=True)]
    all_to_all x8 -> x0, starting transfers between devices: 32 us -> none  [the longest x4 17.6 us: to_cells(): lax.all_to_all(field.reshape(field.shape[0], -1), 'chan', split_axis=1, c...]
    convert_element_type x6 -> x0, other arithmetic: 24 us -> none  [the longest x1 10 us: body(): core(padded_grad, filter_taps, -1).astype(jnp.bfloat16).reshape(slab_shape)]
    dot_general x4 -> x0, matrix products: 12.8 us -> none  [the longest x1 3.83 us: body(): lax.dot_general(full_in, hid_cells, contract_first, preferred_element_typ...]
    all_to_all x8 -> x0, local copies, waits for them, and re-layouts: 10.9 us -> none  [the longest x4 6.25 us: to_channels(): lax.all_to_all(field, 'chan', split_axis=0, concat_axis=1, tiled=True)]
    ppermute x4 -> x0, starting transfers between devices: 5.58 us -> none  [the longest x2 3 us: with_halo(): lax.ppermute(lax.slice_in_dim(block, block.shape[dim] - width, None, axis...]
  transfers between devices with their start and end apart: 14 -> 0, of which waited for: 9 -> 0; matrix products, arithmetic and copies ran while one was open for 13% -> 0% of each run, Pallas kernels for 0% -> 0%
where the time goes in v1:
time: 185 us; the launch traced here: 182 us
  Pallas kernels  171 us (92%)
  local copies, waits for them, and re-layouts  8.83 us (5%)
    pallas_call x1, Pallas kernels, body(): pl.pallas_call(functools.partial(kernel, nc, ns), out_shape=(shape, shape...  171 us
    unnamed x6, local copies, waits for them, and re-layouts  5.48 us

profile of v1, /device:TPU:0, one launch (start us, length us, event | category | flops | bytes accessed | tf_op | source)
XLA Modules:
  0.0 181.8 jit_solution(15527356292278257202)
XLA Ops:
  0.6 0.0 copy-start.1
  0.7 0.1 pad.2.clone
  0.7 0.6 copy-done.1
  1.3 1.4 maximum_maximum_fusion.tap
  2.8 3.3 %copy_bitcast_fusion = (bf16[4,256,512]{2,1,0:T(8,128)(2,1)}, bf16[4,256,512]{2,1,0:T(8,128)(2,1)}) fusion(bf16[256,4,512]{2,1,0:T(4,128)(2,1)} %param.7, bf16[256,4,512]{2,1,0:T(4,128)(2,1)} %param.6), kind=kLoop, calls=%fused_computation | loop fusion | bytes 4194304 | tf_op jit(solution)/shard_map/transpose | solution.py:618
  6.0 170.8 %shard_map.77 = (bf16[4,256,512]{2,1,0:T(8,128)(2,1)}, bf16[4,256,512]{2,1,0:T(8,128)(2,1)}) custom-call(bf16[4,256,512]{2,1,0:T(8,128)(2,1)} %get-tuple-element.9.vol, bf16[4,256,512]{2,1,0:T(8,128)(2,1)} %get-tuple-element.8.grd, bf16[256,1024]{1,0:T(8,128)(2,1)} %win.1, bf16[256,1024]{1,0:T(8,128)(2,1)} %wout.1, f32[32,256]{1,0:T(8,128)} %maximum_maximum_fusion.tap), custom_call_target="tpu_custom_call" | custom-call | flops 4294967296 | bytes 6291456 | tf_op jit(solution)/shard_map/pallas_call | solution.py:579
  176.9 0.0 copy-start
  176.9 3.1 %copy.10 = bf16[256,4,512]{2,1,0:T(4,128)(2,1)} copy(bf16[256,4,512]{2,0,1:T(8,128)(2,1)} %bitcast.9) | data formatting | bytes 2097152
  180.0 0.0 copy-done
  180.0 1.8 copy.11
  (1 shorter events, 0.0 us)
Async XLA Ops:
  0.6 0.7 copy-start.1
  176.9 3.1 %copy-start = (bf16[4,256,512]{2,1,0:T(8,128)(2,1)S(1)}, bf16[4,256,512]{2,1,0:T(8,128)(2,1)}, u32[]{:S(2)}) copy-start(bf16[4,256,512]{2,1,0:T(8,128)(2,1)} %get-tuple-element.5) | copy-start | bytes 3145732

commit v2 on v1

--- a/solution.py
+++ b/solution.py
@@ -225,13 +225,19 @@
             (g, to, s),
         )
 
-    def w2_copy(k, shard, frm, to):
+    across = lax.rem(s + ns // 2, ns)
+    sibling = s + 1 - 2 * lax.rem(s, 2)
+    sibling_across = lax.rem(sibling + ns // 2, ns)
+
+    def w2_copy(k, shard, hop, sending):
+        held = ((s, across), (s, sibling), (across, sibling_across))[hop][0 if sending else 1]
+        rw = part_rows(shard, held)
         return remote(
-            weights.at[k, part_rows(shard, frm), :],
-            weights.at[k, part_rows(shard, frm), :],
-            w2_send.at[k, shard, to],
-            w2_recv.at[k, shard, frm],
-            (g, c, to),
+            weights.at[k, rw, :],
+            weights.at[k, rw, :],
+            w2_send.at[k, shard, hop],
+            w2_recv.at[k, shard, hop],
+            (g, c, across if hop == 0 else sibling),
         )
 
     def tap_copy(frm, to):
@@ -294,8 +300,6 @@
         in_copy(0, c, chan_peer(d)).start()
     for d in range(1, nc):
         w1_copy(1, c, chan_peer(d)).start()
-    for d in range(1, nc):
-        in_copy(1, c, chan_peer(d)).start()
     for copy in own:
         copy.start()
 
@@ -326,20 +330,28 @@
         for d in range(1, nc):
             p = chan_peer(d)
             w1_copy(k, p, c).wait_recv()
-            for e in range(1, ns):
-                w2_copy(k, p, s, space_peer(e)).start()
+            w2_copy(k, p, 0, True).start()
+            w2_copy(k, p, 1, True).start()
+
+    def hand_on(k):
+        for d in range(1, nc):
+            p = chan_peer(d)
+            w2_copy(k, p, 0, False).wait_recv()
+            w2_copy(k, p, 2, True).start()
 
     def await_weights(k):
         for d in range(1, nc):
-            p = chan_peer(d)
-            for e in range(1, ns):
-                w2_copy(k, p, space_peer(e), s).wait_recv()
+            for hop in (1, 2):
+                w2_copy(k, chan_peer(d), hop, False).wait_recv()
 
     spread(0)
     for d in range(1, nc):
         tap_copy(chan_peer(d), c).wait_recv()
     for r in range(nc):
-        tap_s[r * block : (r + 1) * block, 0:TAP_ROWS] = jnp.transpose(tap_t[r])
+        columns = jnp.transpose(tap_t[r])
+        for k in range(28):
+            tap_s[k, r * block : (r + 1) * block, :] = jnp.broadcast_to(columns[:, k : k + 1], (block, LANES))
+    hand_on(0)
     for copy in own:
         copy.wait()
     for d in range(1, nc):
@@ -368,7 +380,7 @@
             pack_y[v, 1, rw, :] = low.astype(bf16)
             return carry
 
-        lax.fori_loop(0, block // step, one, 0)
+        lax.fori_loop(0, block // step, one, 0, unroll=True)
 
     def corner(v, r):
         step = 32
@@ -385,7 +397,7 @@
             pack_c[v, 1, rw, :] = jnp.where(first, low, rolled(high, last)).astype(bf16)
             return carry
 
-        lax.fori_loop(0, block // step, one, 0)
+        lax.fori_loop(0, block // step, one, 0, unroll=True)
 
     def convolve(v, r, finish):
         step = 16
@@ -402,7 +414,6 @@
             high = halo_y[v, 1, rw, :].astype(f32)
             below = halo_c[v, 0, rw, :].astype(f32)
             above = halo_c[v, 1, rw, :].astype(f32)
-            taps = tap_s[rw, :]
             results = [[] for _ in range(planes)]
             for q in range(step // half):
                 cut = slice(q * half, (q + 1) * half)
@@ -426,8 +437,8 @@
                 weight = []
                 for k in range(27):
                     at = k if v == 0 else 26 - k
-                    weight.append(jnp.broadcast_to(taps[cut, at : at + 1], (half, LANES)))
-                bias = jnp.broadcast_to(taps[cut, 27:28], (half, LANES)) if v == 0 else None
+                    weight.append(tap_s[at, pl.ds(pl.multiple_of(r * block + i * step + q * half, half), half), :])
+                bias = tap_s[27, pl.ds(pl.multiple_of(r * block + i * step + q * half, half), half), :] if v == 0 else None
                 for z in range(planes):
                     sums = [None, None, None]
                     for a in range(3):
@@ -445,7 +456,7 @@
                 finish(z, rw, jnp.concatenate(results[z], axis=0))
             return carry
 
-        lax.fori_loop(0, block // step, one, 0)
+        lax.fori_loop(0, block // step, one, 0, unroll=4)
 
     def finish_forward(z, rw, mixed):
         up = 0.5 * (1.0 + lax.erf(mixed * root_half))
@@ -474,19 +485,20 @@
 
         lax.fori_loop(0, nc, run, 0)
 
-    def conv_chunk(v, finish):
+    def conv_chunk(v, finish, begin, end):
         def run(r, carry):
             halo_wait_recv(v, (2, 3, 4, 5), r)
             convolve(v, r, finish)
             return carry
 
-        lax.fori_loop(0, nc, run, 0)
+        lax.fori_loop(begin, end, run, 0)
 
     def out_chunk(k, r, value):
         total = wide(cells, (k,), rows_of(r)).astype(f32) + value
         for z in range(planes):
             stage[k, z, rows_of(r), :] = total[:, z * LANES : (z + 1) * LANES].astype(bf16)
 
+    def out_start(k, r):
         @pl.when(r != c)
         def _():
             out_copy(k, c, r).start()
@@ -518,19 +530,29 @@
 
     def back_chunk(r, carry):
         out_chunk(1, r, flipped(0, r, wide(hid, (), every)))
+        out_start(1, r)
         return carry
 
+    def send_block(r, carry):
+        out_start(0, r)
+        return carry
+
     lax.fori_loop(0, nc, hidden_chunk, 0)
+    for d in range(1, nc):
+        in_copy(1, c, chan_peer(d)).start()
+    corner_chunk(0)
     spread(1)
-    corner_chunk(0)
-    conv_chunk(0, finish_forward)
+    conv_chunk(0, finish_forward, 0, nc // 2)
+    hand_on(1)
+    conv_chunk(0, finish_forward, nc // 2, nc)
     await_weights(1)
     lax.fori_loop(0, nc, block_chunk, 0)
     for d in range(1, nc):
         in_copy(1, chan_peer(d), c).wait_recv()
     lax.fori_loop(0, nc, mix_chunk, 0)
+    lax.fori_loop(0, nc, send_block, 0)
     corner_chunk(1)
-    conv_chunk(1, finish_backward)
+    conv_chunk(1, finish_backward, 0, nc)
     lax.fori_loop(0, nc, back_chunk, 0)
 
     for d in range(1, nc):
@@ -539,8 +561,8 @@
         for k in range(2):
             w1_copy(k, c, p).wait_send()
             in_copy(k, c, p).wait_send()
-            for e in range(1, ns):
-                w2_copy(k, p, s, space_peer(e)).wait_send()
+            for hop in range(3):
+                w2_copy(k, p, hop, True).wait_send()
 
     def drain(r, carry):
         for v in range(2):
@@ -561,7 +583,7 @@
     channels = weight_in.shape[1]
     fits = (
         nc > 1
-        and ns > 1
+        and ns == 4
         and plane == nc * LANES
         and plane == CX * CY
         and planes * CX == LANES
@@ -585,7 +607,7 @@
             pltpu.VMEM((2, planes, channels, LANES), bf16),
             pltpu.VMEM((2, channels, channels), bf16),
             pltpu.VMEM((nc, TAP_ROWS, block), f32),
-            pltpu.VMEM((channels, LANES), f32),
+            pltpu.VMEM((28, channels, LANES), f32),
             pltpu.VMEM((2, planes + 2, channels, LANES), bf16),
             pltpu.VMEM((2, 2, channels, LANES), bf16),
             pltpu.VMEM((2, 2, channels, LANES), bf16),
@@ -599,8 +621,8 @@
             dma((4, nc)),
             dma((2, nc)),
             dma((2, nc)),
-            dma((2, nc, ns)),
-            dma((2, nc, ns)),
+            dma((2, nc, 3)),
+            dma((2, nc, 3)),
             dma((nc,)),
             dma((nc,)),
             dma((2, 6, nc)),

time: 185 us -> 153 us (0.83)
  Pallas kernels: 171 us -> 140 us
    pallas_call x1, Pallas kernels: 171 us -> 140 us  [body(): pl.pallas_call(functools.partial(kernel, nc, ns), out_shape=(shape, shape...]
where the time goes in v2:
time: 153 us; the launch traced here: 151 us
  Pallas kernels  140 us (92%)
  local copies, waits for them, and re-layouts  8.83 us (6%)
    pallas_call x1, Pallas kernels, body(): pl.pallas_call(functools.partial(kernel, nc, ns), out_shape=(shape, shape...  140 us
    unnamed x6, local copies, waits for them, and re-layouts  5.48 us
    transpose x1, local copies, waits for them, and re-layouts, body(): jnp.transpose(out_grad, (1, 0, 2))  3.27 us

profile of v2, /device:TPU:0, one launch (start us, length us, event | category | flops | bytes accessed | tf_op | source)
XLA Modules:
  0.0 151.0 jit_solution(1382466075619278272)
XLA Ops:
  0.6 0.0 copy-start.1
  0.7 0.1 pad.2.clone
  0.7 0.6 copy-done.1
  1.3 1.4 maximum_maximum_fusion.tap
  2.8 3.3 %copy_bitcast_fusion = (bf16[4,256,512]{2,1,0:T(8,128)(2,1)}, bf16[4,256,512]{2,1,0:T(8,128)(2,1)}) fusion(bf16[256,4,512]{2,1,0:T(4,128)(2,1)} %param.7, bf16[256,4,512]{2,1,0:T(4,128)(2,1)} %param.6), kind=kLoop, calls=%fused_computation | loop fusion | bytes 4194304 | tf_op jit(solution)/shard_map/transpose | solution.py:640
  6.0 140.0 %shard_map.77 = (bf16[4,256,512]{2,1,0:T(8,128)(2,1)}, bf16[4,256,512]{2,1,0:T(8,128)(2,1)}) custom-call(bf16[4,256,512]{2,1,0:T(8,128)(2,1)} %get-tuple-element.9.vol, bf16[4,256,512]{2,1,0:T(8,128)(2,1)} %get-tuple-element.8.grd, bf16[256,1024]{1,0:T(8,128)(2,1)} %win.1, bf16[256,1024]{1,0:T(8,128)(2,1)} %wout.1, f32[32,256]{1,0:T(8,128)} %maximum_maximum_fusion.tap), custom_call_target="tpu_custom_call" | custom-call | flops 4294967296 | bytes 6291456 | tf_op jit(solution)/shard_map/pallas_call | solution.py:601
  146.1 0.0 copy-start
  146.1 3.1 %copy.10 = bf16[256,4,512]{2,1,0:T(4,128)(2,1)} copy(bf16[256,4,512]{2,0,1:T(8,128)(2,1)} %bitcast.9) | data formatting | bytes 2097152
  149.2 0.0 copy-done
  149.2 1.8 %copy.11 = bf16[256,4,512]{2,1,0:T(4,128)(2,1)} copy(bf16[256,4,512]{2,0,1:T(8,128)(2,1)S(1)} %bitcast.8) | data formatting | bytes 2097152
  (1 shorter events, 0.0 us)
Async XLA Ops:
  0.6 0.7 copy-start.1
  146.1 3.1 %copy-start = (bf16[4,256,512]{2,1,0:T(8,128)(2,1)S(1)}, bf16[4,256,512]{2,1,0:T(8,128)(2,1)}, u32[]{:S(2)}) copy-start(bf16[4,256,512]{2,1,0:T(8,128)(2,1)} %get-tuple-element.5) | copy-start | bytes 3145732
